TPU v7x, 32 devices: a whole 2x2x4 slice. The times are simulated.
32 devices in a mesh: shard: 2 (over y), tensor: 4 (over z), section: 4 (over x, core).
Axes of the slice: x: 2, y: 2, z: 4, core: 2. Of those that a mesh axis runs over, the one named last changes fastest.
Arguments:
- activations: bfloat16 [4, 4096, 2048], P('section', 'shard'), may hold values from -500 to 500, as said below
- out_grad: bfloat16 [4, 4096, 8192], P('section', 'shard', 'tensor'), may hold values from -30 to 30, as said below
- basis: float32 [4, 2048, 256], P('section', 'shard'), may hold values from -0.125 to 0.125
- first_moment: float32 [4, 256, 8192], P('section', 'shard', 'tensor'), may hold values from -6 to 6
- second_moment: float32 [4, 256, 8192], P('section', 'shard', 'tensor'), may hold values from 0.5 to 2
- gain_partial: float32 [4, 2, 2048], P('section', 'shard'), may hold values from -4096 to 4096
- gain_first: float32 [4, 2048], P('section', 'shard'), may hold values from -6 to 6
- gain_second: float32 [4, 2048], P('section', 'shard'), may hold values from 0.5 to 2
Outputs:
- update: float32 [4, 2048, 8192], P('section', 'shard', 'tensor')
- first_out: float32 [4, 256, 8192], P('section', 'shard', 'tensor')
- second_out: float32 [4, 256, 8192], P('section', 'shard', 'tensor')
- new_basis: float32 [4, 2048, 256], P('section', ('shard', 'tensor'))
- gain_step: float32 [4, 2048], P('section', 'shard')
- gain_first_out: float32 [4, 2048], P('section', 'shard')
- gain_second_out: float32 [4, 2048], P('section', 'shard')
Inputs may be any that keep to these rules, and one draw needn't show every extreme that they name: Real-valued activations whose column scales differ from column to column. `out_grad`: Real-valued gradients whose column scales differ from column to column.
All inputs are finite; a program needn't handle non-finite values.
Results may differ from a plain program's by a relative error of at most 0.0003.
Values sent between devices are 32-bit elements; how exact they have to be, the bound alone decides.
A program may use at most 128 MiB of HBM per device.

v0:
```python
import jax
import jax.numpy as jnp
from jax import lax
from jax.sharding import PartitionSpec as P

D = 2048
FF = 8192
NS_STEPS = 5
STEP = 8


exact_mode = lax.Precision.HIGHEST
beta_one = 0.9
beta_two = 0.999
adam_eps = 1e-08
clip_eps = 1e-06
ns_eps = 1e-07
coef_first = 3.4445
coef_second = -4.775
coef_third = 2.0315


def adam_direction(clipped, first_old, second_old):
    first_new = beta_one * first_old + (1.0 - beta_one) * clipped
    second_new = beta_two * second_old + (1.0 - beta_two) * clipped * clipped
    direction = (
        first_new
        / (1.0 - beta_one**STEP)
        / (jnp.sqrt(second_new / (1.0 - beta_two**STEP)) + adam_eps)
    )
    return (first_new, second_new, direction)


def ns_update(current, gram):
    mixer = coef_second * gram + coef_third * jnp.dot(gram, gram, precision=exact_mode)
    return coef_first * current + jnp.dot(current, mixer, precision=exact_mode)


def gram_of(block):
    local_gram = jnp.dot(block.T, block, precision=exact_mode)
    return lax.psum(local_gram, ("shard", "tensor"))


def shards(
    activations, out_grad, basis, first_moment, second_moment, gain_partial, gain_first, gain_second
):
    tensors = lax.axis_size("tensor")
    shard_pos = lax.axis_index("shard")
    layer_count = activations.shape[0]
    rows_here = basis.shape[1]
    rank_rows = first_moment.shape[1]
    cols_here = out_grad.shape[2]
    layer_index = 0
    tokens_in = activations[layer_index]
    grads_out = out_grad[layer_index]
    basis_here = basis[layer_index]

    def row_term(start, count, tokens_in=tokens_in, grads_out=grads_out):
        return lax.dot_general(
            tokens_in, grads_out, (((0,), (0,)), ((), ())), preferred_element_type=jnp.float32
        )

    grad_block = lax.psum_scatter(
        row_term(jnp.int32(0), lax.axis_size("shard") * rows_here),
        "shard",
        scatter_dimension=0,
        tiled=True,
    )
    part_proj = jnp.dot(basis_here.T, grad_block, precision=exact_mode)
    proj_full, gain_total = lax.psum((part_proj, gain_partial[layer_index, 0]), "shard")
    proj_rows = lax.dynamic_slice_in_dim(proj_full, shard_pos * rank_rows, rank_rows, 0)
    square_sum = jnp.sum(grad_block * grad_block)

    def refresh_term(start, count, grad_block=grad_block, proj_full=proj_full):
        return lax.dot_general(
            grad_block, proj_full, (((1,), (1,)), ((), ())), precision=exact_mode
        )

    refreshed = lax.psum_scatter(
        refresh_term(jnp.int32(0), lax.axis_size("tensor") * (rows_here // tensors)),
        "tensor",
        scatter_dimension=0,
        tiled=True,
    )
    kept_list = [basis_here]
    gain_own = lax.dynamic_slice_in_dim(gain_total, shard_pos * rows_here, rows_here, 0)
    square_sum = square_sum + jnp.sum(gain_own * gain_own) / float(tensors)
    proj_list = [proj_rows]
    gain_list = [gain_own]
    refresh_list = [refreshed]
    total_sq = lax.psum(square_sum, ("shard", "tensor", "section"))
    entry_count = float(lax.axis_size("section") * layer_count * (D * FF + D))
    clip = jnp.minimum(1.0, lax.rsqrt(total_sq / entry_count + clip_eps))
    layer_index = 0
    first_new, second_new, direction = adam_direction(
        clip * proj_list[layer_index], first_moment[layer_index], second_moment[layer_index]
    )
    firsts = [first_new]
    seconds = [second_new]
    kept_basis = kept_list[layer_index]

    def fold_rows(total, piece, start, kept_basis=kept_basis):
        return jnp.dot(kept_basis, piece, precision=exact_mode)

    empty = jnp.zeros((rows_here, cols_here), jnp.float32)
    update_here = fold_rows(
        empty, lax.all_gather(direction, "shard", axis=0, tiled=True), jnp.int32(0)
    )
    updates = [update_here]
    refreshed = refresh_list[layer_index]
    frob = lax.psum(jnp.sum(refreshed * refreshed), ("shard", "tensor"))
    current = refreshed / jnp.sqrt(frob + ns_eps)
    gram = gram_of(current)
    for step_index in range(NS_STEPS):
        current = ns_update(current, gram)
        if step_index + 1 < NS_STEPS:
            gram = gram_of(current)
    bases = [current]
    gain_first_new, gain_second_new, gain_dir = adam_direction(
        clip * gain_list[layer_index], gain_first[layer_index], gain_second[layer_index]
    )
    gain_steps = [gain_dir]
    gain_firsts = [gain_first_new]
    gain_seconds = [gain_second_new]
    return (
        jnp.stack(updates),
        jnp.stack(firsts),
        jnp.stack(seconds),
        jnp.stack(bases),
        jnp.stack(gain_steps),
        jnp.stack(gain_firsts),
        jnp.stack(gain_seconds),
    )


def solution(mesh):
    placed = (
        P("section", "shard", None),
        P("section", "shard", "tensor"),
        P("section", "shard", None),
        P("section", "shard", "tensor"),
        P("section", "shard", "tensor"),
        P("section", "shard", None),
        P("section", "shard"),
        P("section", "shard"),
    )
    return jax.shard_map(
        shards,
        mesh=mesh,
        in_specs=placed,
        out_specs=(
            P("section", "shard", "tensor"),
            P("section", "shard", "tensor"),
            P("section", "shard", "tensor"),
            P("section", ("shard", "tensor"), None),
            P("section", "shard"),
            P("section", "shard"),
            P("section", "shard"),
        ),
        check_vma=False,
    )
```

profile of v0, /device:TPU:0, one launch (start us, length us, event | category | flops | bytes accessed | tf_op | source)
XLA Modules:
  0.0 774.6 jit_solution(11613668346589935621)
XLA Ops:
  7.2 24.3 %fusion = f32[2048,2048]{1,0:T(8,128)} fusion(bf16[1,2048,2048]{2,1,0:T(8,128)(2,1)} %param.9, bf16[1,2048,2048]{2,1,0:T(8,128)(2,1)} %param.8), kind=kOutput, calls=%fused_computation | convolution fusion | flops 17179869184 | bytes 33554432 | tf_op jit(solution)/shard_map/dot_general | solution.py:59
  31.6 191.9 %reduce-scatter.3.cloned.1.call-done = f32[1024,2048]{1,0:T(8,128)} async-done(((f32[2048,2048]{1,0:T(8,128)}), f32[1024,2048]{1,0:T(8,128)}) %reduce-scatter.3.cloned.1.call-update) | async-done | bytes 8388624 | tf_op jit(solution)/shard_map/reduce_scatter | solution.py:63
  223.6 16.5 %convolution_bitcast_fusion.1 = f32[256,2048]{0,1:T(8,128)} fusion(f32[1024,2048]{1,0:T(8,128)} %reduce-scatter.3.cloned.1.call-done, f32[1,1024,256]{2,1,0:T(8,128)S(1)} %copy-done), kind=kOutput, calls=%fused_computation.5 | convolution fusion | flops 6442450944 | bytes 11534336 | tf_op jit(solution)/shard_map/dot_general | solution.py:69
  240.4 62.9 %all-reduce.7.cloned.1.call-done = f32[256,2048]{0,1:T(8,128)} async-done(((f32[256,2048]{0,1:T(8,128)}), f32[256,2048]{0,1:T(8,128)}) %all-reduce.7.cloned.1.call-update) | async-done | bytes 2097168 | tf_op jit(solution)/shard_map/psum | solution.py:70
  303.2 10.6 %fusion.17 = f32[1024,256]{1,0:T(8,128)} fusion(f32[1024,2048]{1,0:T(8,128)} %reduce-scatter.3.cloned.1.call-done, f32[256,2048]{0,1:T(8,128)} %all-reduce.7.cloned.1.call-done), kind=kOutput, calls=%fused_computation.41 | convolution fusion | flops 6442450944 | bytes 11534336 | tf_op jit(solution)/shard_map/dot_general | solution.py:75
  313.8 27.2 %reduce-scatter.5.cloned.1.call-done = f32[256,256]{1,0:T(8,128)} async-done(((f32[1024,256]{1,0:T(8,128)}), f32[256,256]{1,0:T(8,128)}) %reduce-scatter.5.cloned.1.call-update) | async-done | bytes 262160 | tf_op jit(solution)/shard_map/reduce_scatter | solution.py:79
  341.1 1.6 multiply_reduce_fusion.1
  342.7 19.8 %psum.66 = f32[]{:T(128)} all-reduce(f32[]{:T(128)} %multiply_reduce_fusion.1), channel_id=1, replica_groups=mesh['shard'=2,'tensor'=4,'section'=4] {'shard','tensor'}, use_global_device_ids=true, to_apply=%region_8.0 | all-reduce | flops 1 | bytes 8 | tf_op jit(solution)/shard_map/psum | solution.py:111
  363.2 2.3 fusion.14
  365.6 68.3 %all-reduce.9.cloned.1.call-done = f32[256,256]{1,0:T(8,128)} async-done(((f32[256,256]{1,0:T(8,128)}), f32[256,256]{1,0:T(8,128)}) %all-reduce.9.cloned.1.call-update) | async-done | bytes 262160 | tf_op jit(solution)/shard_map/psum | solution.py:41
  439.5 2.7 copy.16
  442.2 5.0 psum.63
  448.4 59.7 %all-reduce.11.cloned.1.call-done = f32[256,256]{1,0:T(8,128)} async-done(((f32[256,256]{1,0:T(8,128)}), f32[256,256]{1,0:T(8,128)}) %all-reduce.11.cloned.1.call-update) | async-done | bytes 262160 | tf_op jit(solution)/shard_map/psum | solution.py:41
  512.1 6.1 multiply_reduce_fusion
  518.9 39.6 %psum.64 = f32[]{:T(128)} all-reduce(f32[]{:T(128)S(6)} %add.92), channel_id=1, replica_groups=mesh['shard'=2,'tensor'=4,'section'=4] {'shard','tensor','section'}, use_global_device_ids=true, to_apply=%region_4.0 | all-reduce | flops 1 | bytes 8 | tf_op jit(solution)/shard_map/psum | solution.py:91
  559.3 23.0 %all-reduce.13.cloned.1.call-done = f32[256,256]{1,0:T(8,128)} async-done(((f32[256,256]{1,0:T(8,128)}), f32[256,256]{1,0:T(8,128)}) %all-reduce.13.cloned.1.call-update) | async-done | bytes 262160 | tf_op jit(solution)/shard_map/psum | solution.py:41
  586.6 3.9 fusion.13
  591.4 2.5 copy.18
  593.9 2.5 copy.19
  596.5 60.1 %all-reduce.15.cloned.1.call-done = f32[256,256]{1,0:T(8,128)} async-done(((f32[256,256]{1,0:T(8,128)}), f32[256,256]{1,0:T(8,128)}) %all-reduce.15.cloned.1.call-update) | async-done | bytes 262160 | tf_op jit(solution)/shard_map/psum | solution.py:41
  659.8 30.8 %all-gather.2.cloned.1.call-done = f32[256,2048]{0,1:T(8,128)} async-done(((f32[128,2048]{0,1:T(8,128)}), f32[256,2048]{0,1:T(8,128)}) %all-gather.2.cloned.1.call-update) | async-done | bytes 2097168 | tf_op jit(solution)/shard_map/all_gather | solution.py:107
  690.6 10.2 %convolution_bitcast_fusion = f32[1,1024,2048]{1,2,0:T(8,128)} fusion(f32[256,2048]{0,1:T(8,128)} %all-gather.2.cloned.1.call-done, f32[1,1024,256]{2,1,0:T(8,128)S(1)} %copy-done), kind=kOutput, calls=%fused_computation.4 | convolution fusion | flops 6442450944 | bytes 11534336 | tf_op jit(solution)/shard_map/dot_general | solution.py:103
  700.8 9.1 %copy.17 = f32[1,1024,2048]{2,1,0:T(8,128)} copy(f32[1,1024,2048]{1,2,0:T(8,128)} %convolution_bitcast_fusion) | data formatting | bytes 16777216
  709.9 55.5 %all-reduce.17.cloned.1.call-done = f32[256,256]{1,0:T(8,128)} async-done(((f32[256,256]{1,0:T(8,128)}), f32[256,256]{1,0:T(8,128)}) %all-reduce.17.cloned.1.call-update) | async-done | bytes 262160 | tf_op jit(solution)/shard_map/psum | solution.py:41
  (51 shorter events, 21.6 us)
Async XLA Ops:
  7.2 216.4 %copy-start = (f32[1,1024,256]{2,1,0:T(8,128)S(1)}, f32[1,1024,256]{2,1,0:T(8,128)}, u32[]{:S(2)}) copy-start(f32[1,1024,256]{2,1,0:T(8,128)} %param.10) | copy-start | bytes 3145732
  7.2 216.4 %reduce-scatter.3.cloned.1.call-start = ((), (), s32[]{:S(2)}) async-start(), calls=%async_computation.2 | async-start | bytes 25165824 | tf_op jit(solution)/shard_map/reduce_scatter | solution.py:63
  31.6 271.6 %all-reduce.7.cloned.1.call-start = ((), (), s32[]{:S(2)}) async-start(), calls=%async_computation.3 | async-start | bytes 4194304 | tf_op jit(solution)/shard_map/psum | solution.py:70
  240.1 198.1 %copy-start.3 = (f32[1,128,2048]{2,1,0:T(8,128)S(1)}, f32[1,128,2048]{2,1,0:T(8,128)}, u32[]{:S(2)}) copy-start(f32[1,128,2048]{2,1,0:T(8,128)} %param.11) | copy-start | bytes 3145732
  240.1 101.0 %reduce-scatter.5.cloned.1.call-start = ((), (), s32[]{:S(2)}) async-start(), calls=%async_computation.5 | async-start | bytes 1310720 | tf_op jit(solution)/shard_map/reduce_scatter | solution.py:79
  313.8 128.4 %copy-start.4 = (f32[1,1,2048]{2,1,0:T(1,128)S(1)}, f32[1,1,2048]{2,1,0:T(1,128)}, u32[]{:S(2)}) copy-start(f32[1,1,2048]{2,1,0:T(1,128)} %param.13) | copy-start | bytes 24580
  313.8 120.1 %all-reduce.9.cloned.1.call-start = ((), (), s32[]{:S(2)}) async-start(), calls=%async_computation.6 | async-start | bytes 524288 | tf_op jit(solution)/shard_map/psum | solution.py:41
  365.6 142.6 %all-reduce.11.cloned.1.call-start = ((), (), s32[]{:S(2)}) async-start(), calls=%async_computation.7 | async-start | bytes 524288 | tf_op jit(solution)/shard_map/psum | solution.py:41
  438.1 144.1 %all-reduce.13.cloned.1.call-start = ((), (), s32[]{:S(2)}) async-start(), calls=%async_computation.8 | async-start | bytes 524288 | tf_op jit(solution)/shard_map/psum | solution.py:41
  439.5 147.0 %copy-start.1 = (f32[256,2048]{0,1:T(8,128)S(1)}, f32[256,2048]{0,1:T(8,128)}, u32[]{:S(2)}) copy-start(f32[256,2048]{0,1:T(8,128)} %all-reduce.7.cloned.1.call-done) | copy-start | bytes 6291460
  510.0 0.7 copy-start.2
  512.1 78.7 %copy-start.5 = (f32[1,1024]{1,0:T(1,128)S(1)}, f32[1,1024]{1,0:T(1,128)}, u32[]{:S(2)}) copy-start(f32[1,1024]{1,0:T(1,128)} %param.14) | copy-start | bytes 12292
  512.1 78.7 %copy-start.6 = (f32[1,1024]{1,0:T(1,128)S(1)}, f32[1,1024]{1,0:T(1,128)}, u32[]{:S(2)}) copy-start(f32[1,1024]{1,0:T(1,128)} %param.15) | copy-start | bytes 12292
  512.1 144.5 %all-reduce.15.cloned.1.call-start = ((), (), s32[]{:S(2)}) async-start(), calls=%async_computation.9 | async-start | bytes 524288 | tf_op jit(solution)/shard_map/psum | solution.py:41
  586.5 104.1 %all-gather.2.cloned.1.call-start = ((), (), s32[]{:S(2)}) async-start(), calls=%async_computation.4 | async-start | bytes 3145728 | tf_op jit(solution)/shard_map/all_gather | solution.py:107
  590.5 175.0 %all-reduce.17.cloned.1.call-start = ((), (), s32[]{:S(2)}) async-start(), calls=%async_computation.10 | async-start | bytes 524288 | tf_op jit(solution)/shard_map/psum | solution.py:41
Sparse Core Ops, SparseCore 0:
  31.7 191.8 reduce-scatter.2
  240.2 62.9 all-reduce.6
  313.9 27.1 reduce-scatter.4
  365.7 68.1 all-reduce.8
  438.3 69.8 all-reduce.10
  512.3 69.8 all-reduce.12
  586.6 69.9 all-reduce.14
  658.2 32.3 all-gather.1
  694.9 70.5 all-reduce.16
where the time goes:
time: 775 us
  waiting for transfers between devices  580 us (75%)
  matrix products  81.3 us (10%)
  blocking collectives  64.4 us (8%)
  local copies, waits for them, and re-layouts  18.9 us (2%)
  between operations  16.7 us (2%)
  other arithmetic  12.9 us (2%)
    psum x5, waiting for transfers between devices, gram_of(): return lax.psum(local_gram, ('shard', 'tensor'))  267 us
    reduce_scatter x1, waiting for transfers between devices, shards(): lax.psum_scatter(row_term(jnp.int32(0), lax.axis_size('shard') * rows_her...  192 us
    psum x1, waiting for transfers between devices, shards(): lax.psum((part_proj, gain_partial[layer_index, 0]), 'shard')  62.9 us
    psum x1, blocking collectives, shards(): total_sq = lax.psum(square_sum, ('shard', 'tensor', 'section'))  39.6 us
    all_gather x1, waiting for transfers between devices, shards(): lax.all_gather(direction, 'shard', axis=0, tiled=True)  30.8 us
    reduce_scatter x1, waiting for transfers between devices, shards(): lax.psum_scatter(refresh_term(jnp.int32(0), lax.axis_size('tensor') * (ro...  27.2 us
    dot_general x1, matrix products, row_term(): lax.dot_general(tokens_in, grads_out, (((0,), (0,)), ((), ())), preferred...  24.3 us
    psum x1, blocking collectives, shards(): frob = lax.psum(jnp.sum(refreshed * refreshed), ('shard', 'tensor'))  19.8 us
  transfers between devices with their start and end apart: 9, of which 9 were waited for; matrix products, arithmetic and copies ran while one was open for 6% of the time, Pallas kernels for 0%

commit v1 on v0

--- a/solution.py
+++ b/solution.py
@@ -31,14 +31,25 @@
     return (first_new, second_new, direction)
 
 
-def ns_update(current, gram):
-    mixer = coef_second * gram + coef_third * jnp.dot(gram, gram, precision=exact_mode)
-    return coef_first * current + jnp.dot(current, mixer, precision=exact_mode)
+def exact_dot(left, right):
+    return jnp.dot(left, right, precision=exact_mode)
 
 
-def gram_of(block):
-    local_gram = jnp.dot(block.T, block, precision=exact_mode)
-    return lax.psum(local_gram, ("shard", "tensor"))
+def ns_mixer(raw_gram):
+    size = raw_gram.shape[0]
+    same = lax.broadcasted_iota(jnp.int32, (size, size), 0) == lax.broadcasted_iota(
+        jnp.int32, (size, size), 1
+    )
+    frob = jnp.sum(jnp.where(same, raw_gram, 0.0))
+    gram = raw_gram / (frob + ns_eps)
+    total = None
+    for step_index in range(NS_STEPS):
+        mixer = coef_second * gram + coef_third * exact_dot(gram, gram)
+        mixer = mixer + jnp.where(same, coef_first, 0.0)
+        total = mixer if total is None else exact_dot(total, mixer)
+        if step_index + 1 < NS_STEPS:
+            gram = exact_dot(mixer, exact_dot(gram, mixer))
+    return total, lax.rsqrt(frob + ns_eps)
 
 
 def shards(
@@ -108,13 +119,11 @@
     )
     updates = [update_here]
     refreshed = refresh_list[layer_index]
-    frob = lax.psum(jnp.sum(refreshed * refreshed), ("shard", "tensor"))
-    current = refreshed / jnp.sqrt(frob + ns_eps)
-    gram = gram_of(current)
-    for step_index in range(NS_STEPS):
-        current = ns_update(current, gram)
-        if step_index + 1 < NS_STEPS:
-            gram = gram_of(current)
+    raw_gram = lax.psum(
+        jnp.dot(refreshed.T, refreshed, precision=exact_mode), ("shard", "tensor")
+    )
+    mixer, scale = ns_mixer(raw_gram)
+    current = exact_dot(refreshed * scale, mixer)
     bases = [current]
     gain_first_new, gain_second_new, gain_dir = adam_direction(
         clip * gain_list[layer_index], gain_first[layer_index], gain_second[layer_index]

time: 775 us -> 505 us (0.65)
  waiting for transfers between devices: 580 us -> 336 us
  blocking collectives: 64.4 us -> 44.4 us
    psum x5 -> x1, waiting for transfers between devices: 267 us -> 55.4 us  [shards(): lax.psum(jnp.dot(refreshed.T, refreshed, precision=exact_mode), ('shard',...]
    reduce_scatter x1, waiting for transfers between devices: 27.2 us -> 0.01 us  [shards(): lax.psum_scatter(refresh_term(jnp.int32(0), lax.axis_size('tensor') * (ro...]
    psum x1 -> x0, blocking collectives: 19.8 us -> none  [shards(): frob = lax.psum(jnp.sum(refreshed * refreshed), ('shard', 'tensor'))]
    dot_general x15 -> x19, matrix products: 19.7 us -> 12.2 us  [the longest x18 9.84 us: exact_dot(): return jnp.dot(left, right, precision=exact_mode)]
    unnamed x19 -> x17, local copies, waits for them, and re-layouts: 18.9 us -> 19.4 us
  transfers between devices with their start and end apart: 9 -> 5, of which waited for: 9 -> 4; matrix products, arithmetic and copies ran while one was open for 6% -> 9% of each run, Pallas kernels for 0% -> 0%
where the time goes in v1:
time: 505 us; the launch traced here: 504 us
  waiting for transfers between devices  336 us (67%)
  matrix products  73.9 us (15%)
  blocking collectives  44.4 us (9%)
  local copies, waits for them, and re-layouts  19.4 us (4%)
  between operations  16.7 us (3%)
  other arithmetic  12.9 us (3%)
    reduce_scatter x1, waiting for transfers between devices, shards(): lax.psum_scatter(row_term(jnp.int32(0), lax.axis_size('shard') * rows_her...  192 us
    psum x1, waiting for transfers between devices, shards(): lax.psum((part_proj, gain_partial[layer_index, 0]), 'shard')  62.9 us
    psum x1, waiting for transfers between devices, shards(): lax.psum(jnp.dot(refreshed.T, refreshed, precision=exact_mode), ('shard',...  55.4 us
    psum x1, blocking collectives, shards(): total_sq = lax.psum(square_sum, ('shard', 'tensor', 'section'))  39.4 us
    all_gather x1, waiting for transfers between devices, shards(): lax.all_gather(direction, 'shard', axis=0, tiled=True)  25.8 us
    dot_general x1, matrix products, row_term(): lax.dot_general(tokens_in, grads_out, (((0,), (0,)), ((), ())), preferred...  24.3 us
    unnamed x17, local copies, waits for them, and re-layouts  19.4 us
    dot_general x1, matrix products, shards(): part_proj = jnp.dot(basis_here.T, grad_block, precision=exact_mode)  16.5 us
  transfers between devices with their start and end apart: 5, of which 4 were waited for; matrix products, arithmetic and copies ran while one was open for 9% of the time, Pallas kernels for 0%

profile of v1, /device:TPU:0, one launch (start us, length us, event | category | flops | bytes accessed | tf_op | source)
XLA Modules:
  0.0 503.8 jit_solution(7333105966687494822)
XLA Ops:
  7.2 24.3 %fusion = f32[2048,2048]{1,0:T(8,128)} fusion(bf16[1,2048,2048]{2,1,0:T(8,128)(2,1)} %param.9, bf16[1,2048,2048]{2,1,0:T(8,128)(2,1)} %param.8), kind=kOutput, calls=%fused_computation | convolution fusion | flops 17179869184 | bytes 33554432 | tf_op jit(solution)/shard_map/dot_general | solution.py:70
  31.6 191.9 %reduce-scatter.3.cloned.1.call-done = f32[1024,2048]{1,0:T(8,128)} async-done(((f32[2048,2048]{1,0:T(8,128)}), f32[1024,2048]{1,0:T(8,128)}) %reduce-scatter.3.cloned.1.call-update) | async-done | bytes 8388624 | tf_op jit(solution)/shard_map/reduce_scatter | solution.py:74
  223.6 16.5 %convolution_bitcast_fusion.1 = f32[256,2048]{0,1:T(8,128)} fusion(f32[1024,2048]{1,0:T(8,128)} %reduce-scatter.3.cloned.1.call-done, f32[1,1024,256]{2,1,0:T(8,128)S(1)} %copy-done), kind=kOutput, calls=%fused_computation.5 | convolution fusion | flops 6442450944 | bytes 11534336 | tf_op jit(solution)/shard_map/dot_general | solution.py:80
  240.4 62.9 %all-reduce.3.cloned.1.call-done = f32[256,2048]{0,1:T(8,128)} async-done(((f32[256,2048]{0,1:T(8,128)}), f32[256,2048]{0,1:T(8,128)}) %all-reduce.3.cloned.1.call-update) | async-done | bytes 2097168 | tf_op jit(solution)/shard_map/psum | solution.py:81
  303.2 10.6 %fusion.23 = f32[1024,256]{1,0:T(8,128)} fusion(f32[1024,2048]{1,0:T(8,128)} %reduce-scatter.3.cloned.1.call-done, f32[256,2048]{0,1:T(8,128)} %all-reduce.3.cloned.1.call-done), kind=kOutput, calls=%fused_computation.44 | convolution fusion | flops 6442450944 | bytes 11534336 | tf_op jit(solution)/shard_map/dot_general | solution.py:86
  313.9 2.7 copy.15
  316.5 2.5 copy.16
  319.1 5.0 psum.28
  324.1 0.6 multiply_reduce_fusion.1
  325.3 6.2 %multiply_reduce_fusion = f32[]{:T(128)} fusion(f32[1024,2048]{1,0:T(8,128)} %reduce-scatter.3.cloned.1.call-done), kind=kLoop, calls=%fused_computation.3 | loop fusion | flops 4194303 | bytes 8388612 | tf_op jit(solution)/shard_map/reduce_sum | solution.py:83
  332.2 39.4 %psum.29 = f32[]{:T(128)} all-reduce(f32[]{:T(128)S(6)} %add.83), channel_id=1, replica_groups=mesh['shard'=2,'tensor'=4,'section'=4] {'shard','tensor','section'}, use_global_device_ids=true, to_apply=%region_4.0 | all-reduce | flops 1 | bytes 8 | tf_op jit(solution)/shard_map/psum | solution.py:102
  372.2 3.9 fusion.18
  376.5 0.6 add_divide_fusion.1
  377.1 2.5 copy.18
  379.6 2.5 copy.19
  382.1 2.4 fusion.24
  384.5 25.8 %all-gather.2.cloned.1.call-done = f32[256,2048]{0,1:T(8,128)} async-done(((f32[128,2048]{0,1:T(8,128)}), f32[256,2048]{0,1:T(8,128)}) %all-gather.2.cloned.1.call-update) | async-done | bytes 2097168 | tf_op jit(solution)/shard_map/all_gather | solution.py:118
  410.3 10.2 %convolution_bitcast_fusion = f32[1,1024,2048]{1,2,0:T(8,128)} fusion(f32[256,2048]{0,1:T(8,128)} %all-gather.2.cloned.1.call-done, f32[1,1024,256]{2,1,0:T(8,128)S(1)} %copy-done), kind=kOutput, calls=%fused_computation.4 | convolution fusion | flops 6442450944 | bytes 11534336 | tf_op jit(solution)/shard_map/dot_general | solution.py:114
  420.5 9.1 %copy.17 = f32[1,1024,2048]{2,1,0:T(8,128)} copy(f32[1,1024,2048]{1,2,0:T(8,128)} %convolution_bitcast_fusion) | data formatting | bytes 16777216
  429.7 55.4 %all-reduce.5.cloned.1.call-done = f32[256,256]{1,0:T(8,128)} async-done(((f32[256,256]{1,0:T(8,128)}), f32[256,256]{1,0:T(8,128)}) %all-reduce.5.cloned.1.call-update) | async-done | bytes 262160 | tf_op jit(solution)/shard_map/psum | solution.py:122
  485.0 1.6 select_reduce_fusion
  487.3 1.7 fusion.8
  489.0 1.3 fusion.20
  496.2 1.1 convolution_bitcast_fusion.2
  (40 shorter events, 6.4 us)
Async XLA Ops:
  7.2 216.4 %copy-start = (f32[1,1024,256]{2,1,0:T(8,128)S(1)}, f32[1,1024,256]{2,1,0:T(8,128)}, u32[]{:S(2)}) copy-start(f32[1,1024,256]{2,1,0:T(8,128)} %param.10) | copy-start | bytes 3145732
  7.2 216.4 %reduce-scatter.3.cloned.1.call-start = ((), (), s32[]{:S(2)}) async-start(), calls=%async_computation.2 | async-start | bytes 25165824 | tf_op jit(solution)/shard_map/reduce_scatter | solution.py:74
  31.6 271.6 %all-reduce.3.cloned.1.call-start = ((), (), s32[]{:S(2)}) async-start(), calls=%async_computation.3 | async-start | bytes 4194304 | tf_op jit(solution)/shard_map/psum | solution.py:81
  240.1 79.0 %copy-start.3 = (f32[1,1,2048]{2,1,0:T(1,128)S(1)}, f32[1,1,2048]{2,1,0:T(1,128)}, u32[]{:S(2)}) copy-start(f32[1,1,2048]{2,1,0:T(1,128)} %param.13) | copy-start | bytes 24580
  240.1 142.0 %reduce-scatter.5.cloned.1.call-start = ((), (), s32[]{:S(2)}) async-start(), calls=%async_computation.5 | async-start | bytes 1310720 | tf_op jit(solution)/shard_map/reduce_scatter | solution.py:90
  313.8 58.4 %copy-start.1 = (f32[256,2048]{0,1:T(8,128)S(1)}, f32[256,2048]{0,1:T(8,128)}, u32[]{:S(2)}) copy-start(f32[256,2048]{0,1:T(8,128)} %all-reduce.3.cloned.1.call-done) | copy-start | bytes 6291460
  313.8 96.5 %all-gather.2.cloned.1.call-start = ((), (), s32[]{:S(2)}) async-start(), calls=%async_computation.4 | async-start | bytes 3145728 | tf_op jit(solution)/shard_map/all_gather | solution.py:118
  319.1 57.3 %copy-start.4 = (f32[1,1024]{1,0:T(1,128)S(1)}, f32[1,1024]{1,0:T(1,128)}, u32[]{:S(2)}) copy-start(f32[1,1024]{1,0:T(1,128)} %param.14) | copy-start | bytes 12292
  319.1 57.4 %copy-start.5 = (f32[1,1024]{1,0:T(1,128)S(1)}, f32[1,1024]{1,0:T(1,128)}, u32[]{:S(2)}) copy-start(f32[1,1024]{1,0:T(1,128)} %param.15) | copy-start | bytes 12292
  376.1 108.9 %all-reduce.5.cloned.1.call-start = ((), (), s32[]{:S(2)}) async-start(), calls=%async_computation.6 | async-start | bytes 524288 | tf_op jit(solution)/shard_map/psum | solution.py:122
  429.7 66.6 %copy-start.2 = (f32[256,256]{1,0:T(8,128)S(1)}, f32[256,256]{1,0:T(8,128)}, u32[]{:S(2)}) copy-start(f32[256,256]{1,0:T(8,128)} %reduce-scatter.5.cloned.1.call-done) | copy-start | bytes 786436
Sparse Core Ops, SparseCore 0:
  31.7 191.8 reduce-scatter.2
  240.2 62.9 all-reduce.2
  313.9 27.1 reduce-scatter.4
  376.3 34.0 all-gather.1
  414.4 70.5 all-reduce.4

commit v2 on v1

--- a/solution.py
+++ b/solution.py
@@ -1,10 +1,15 @@
+import functools
+
 import jax
 import jax.numpy as jnp
 from jax import lax
 from jax.sharding import PartitionSpec as P
+from jax.experimental import pallas as pl
+from jax.experimental.pallas import tpu as pltpu
 
 D = 2048
 FF = 8192
+LAYERS = 4
 NS_STEPS = 5
 STEP = 8
 
@@ -142,6 +147,447 @@
     )
 
 
+MESH = pl.DeviceIdType.MESH
+CHUNK = 256
+BLOCK = 256
+
+
+def exact_dims(left, right, dims):
+    return lax.dot_general(
+        left, right, (dims, ((), ())), precision=exact_mode, preferred_element_type=jnp.float32
+    )
+
+
+def exchange_kernel(
+    tokens_ref,
+    grads_ref,
+    basis_t_ref,
+    gain_ref,
+    proj_ref,
+    rows_ref,
+    square_ref,
+    gain_out_ref,
+    sent,
+    landed,
+    own,
+    part,
+    part_landed,
+    gain_landed,
+    grad_send,
+    grad_recv,
+    part_send,
+    part_recv,
+    gain_send,
+    gain_recv,
+):
+    chunks, rows_here, width = own.shape
+    me = lax.axis_index("shard")
+    other = 1 - me
+    barrier = pltpu.get_barrier_semaphore()
+    pl.semaphore_signal(barrier, inc=1, device_id={"shard": other}, device_id_type=MESH)
+    pl.semaphore_wait(barrier, 1)
+
+    def remote(source, target, send, recv):
+        return pltpu.make_async_remote_copy(
+            src_ref=source,
+            dst_ref=target,
+            send_sem=send,
+            recv_sem=recv,
+            device_id={"shard": other},
+            device_id_type=MESH,
+        )
+
+    def grad_copy(c):
+        return remote(sent.at[c], landed.at[c], grad_send.at[c], grad_recv.at[c])
+
+    def part_copy(c):
+        return remote(part.at[c], part_landed.at[c], part_send.at[c], part_recv.at[c])
+
+    gain_copy = remote(gain_ref, gain_landed, gain_send, gain_recv)
+    gain_copy.start()
+
+    def multiply(target, half, c):
+        columns = pl.ds(pl.multiple_of(c * width, width), width)
+
+        @pl.loop(0, rows_here // BLOCK)
+        def _(m):
+            start = pl.multiple_of(half * rows_here + m * BLOCK, BLOCK)
+            target[c, pl.ds(pl.multiple_of(m * BLOCK, BLOCK), BLOCK), :] = lax.dot_general(
+                tokens_ref[:, pl.ds(start, BLOCK)],
+                grads_ref[:, columns],
+                (((0,), (0,)), ((), ())),
+                preferred_element_type=jnp.float32,
+            )
+
+    @pl.loop(0, chunks)
+    def _(c):
+        multiply(sent, other, c)
+        grad_copy(c).start()
+
+    @pl.loop(0, chunks)
+    def _(c):
+        multiply(own, me, c)
+
+    rows_ref[...] = jnp.zeros_like(rows_ref)
+    square_ref[...] = jnp.zeros_like(square_ref)
+
+    def refresh(c):
+        part_copy(c).wait_recv()
+        proj = part[c] + part_landed[c]
+        proj_ref[c] = proj
+
+        @pl.loop(0, rows_here // BLOCK)
+        def _(m):
+            block = pl.ds(pl.multiple_of(m * BLOCK, BLOCK), BLOCK)
+            rows_ref[block, :] += exact_dims(own[c, block, :], proj, ((1,), (1,)))
+
+    lag = min(4, chunks)
+
+    @pl.loop(0, chunks)
+    def _(c):
+        grad_copy(c).wait_recv()
+
+        @pl.loop(0, rows_here // BLOCK)
+        def _(m):
+            block = pl.ds(pl.multiple_of(m * BLOCK, BLOCK), BLOCK)
+            total = own[c, block, :] + landed[c, block, :]
+            own[c, block, :] = total
+            square_ref[...] += jnp.sum((total * total).reshape(BLOCK // 8, 8, width), axis=0)
+
+        part[c] = exact_dims(basis_t_ref[...], own[c], ((1,), (0,)))
+        part_copy(c).start()
+
+        @pl.when(c >= lag)
+        def _():
+            refresh(c - lag)
+
+    @pl.loop(chunks - lag, chunks)
+    def _(c):
+        refresh(c)
+
+    gain_copy.wait_recv()
+    gain_out_ref[...] = gain_ref[...] + gain_landed[...]
+    gain_copy.wait_send()
+
+    @pl.loop(0, chunks)
+    def _(c):
+        grad_copy(c).wait_send()
+        part_copy(c).wait_send()
+
+
+def exchange(tokens_in, grads_out, basis_t, gain):
+    rank, rows_here = basis_t.shape
+    cols = grads_out.shape[1]
+    chunks = cols // CHUNK
+    vmem = pl.BlockSpec(memory_space=pltpu.VMEM)
+    f32 = jnp.float32
+    flops = 2 * tokens_in.shape[0] * tokens_in.shape[1] * cols + 24 * rank * rows_here * cols
+    return pl.pallas_call(
+        exchange_kernel,
+        out_shape=(
+            jax.ShapeDtypeStruct((chunks, rank, CHUNK), f32),
+            jax.ShapeDtypeStruct((rows_here, rank), f32),
+            jax.ShapeDtypeStruct((8, CHUNK), f32),
+            jax.ShapeDtypeStruct(gain.shape, f32),
+        ),
+        in_specs=[vmem] * 4,
+        out_specs=(vmem,) * 4,
+        scratch_shapes=[
+            pltpu.VMEM((chunks, rows_here, CHUNK), f32),
+            pltpu.VMEM((chunks, rows_here, CHUNK), f32),
+            pltpu.VMEM((chunks, rows_here, CHUNK), f32),
+            pltpu.VMEM((chunks, rank, CHUNK), f32),
+            pltpu.VMEM((chunks, rank, CHUNK), f32),
+            pltpu.VMEM(gain.shape, f32),
+            pltpu.SemaphoreType.DMA((chunks,)),
+            pltpu.SemaphoreType.DMA((chunks,)),
+            pltpu.SemaphoreType.DMA((chunks,)),
+            pltpu.SemaphoreType.DMA((chunks,)),
+            pltpu.SemaphoreType.DMA,
+            pltpu.SemaphoreType.DMA,
+        ],
+        compiler_params=pltpu.CompilerParams(
+            collective_id=0, has_side_effects=True, vmem_limit_bytes=60 * 2**20
+        ),
+        cost_estimate=pl.CostEstimate(flops=flops, bytes_accessed=2**25, transcendentals=0),
+        name="exchange",
+    )(tokens_in, grads_out, basis_t, gain)
+
+
+def finish_kernel(
+    axes,
+    proj_ref,
+    rows_ref,
+    square_ref,
+    gain_ref,
+    first_ref,
+    second_ref,
+    gain_first_ref,
+    gain_second_ref,
+    first_out,
+    second_out,
+    direction_out,
+    basis_out,
+    gain_step_out,
+    gain_first_out,
+    gain_second_out,
+    row_slots,
+    one_square,
+    section_slots,
+    group_square,
+    group_slots,
+    dir_own,
+    dir_landed,
+    gram,
+    gram_slots,
+    gram_part,
+    gram_full,
+    row_sems,
+    section_sems,
+    group_sems,
+    dir_sems,
+    gram_sems,
+    full_sems,
+):
+    shards_n, tensors_n, sections_n, entry_count = axes
+    group_n = shards_n * tensors_n
+    chunks, rank, width = proj_ref.shape
+    rank_rows = rank // shards_n
+    shard_pos = lax.axis_index("shard")
+    tensor_pos = lax.axis_index("tensor")
+    section_pos = lax.axis_index("section")
+    me = shard_pos * tensors_n + tensor_pos
+    piece = rank // group_n
+
+    def in_group(step):
+        peer = lax.rem(me + step, group_n)
+        return peer, {"shard": peer // tensors_n, "tensor": lax.rem(peer, tensors_n)}
+
+    def in_section(step):
+        return {"section": lax.rem(section_pos + step, sections_n)}
+
+    barrier = pltpu.get_barrier_semaphore()
+    for step in range(1, group_n):
+        pl.semaphore_signal(barrier, inc=1, device_id=in_group(step)[1], device_id_type=MESH)
+    for step in range(1, sections_n):
+        pl.semaphore_signal(barrier, inc=1, device_id=in_section(step), device_id_type=MESH)
+    pl.semaphore_wait(barrier, group_n - 1 + sections_n - 1)
+
+    def remote(source, target, sems, k, where):
+        return pltpu.make_async_remote_copy(
+            src_ref=source,
+            dst_ref=target,
+            send_sem=sems.at[0, k],
+            recv_sem=sems.at[1, k],
+            device_id=where,
+            device_id_type=MESH,
+        )
+
+    gain_squares = gain_ref[...] * gain_ref[...]
+    share = jnp.sum(gain_squares) / float(group_n)
+    local = jnp.sum(square_ref[...]) + share
+    one_square[...] = jnp.full(one_square.shape, local, jnp.float32)
+    section_copies = []
+    for step in range(1, sections_n):
+        copy = remote(
+            one_square, section_slots.at[section_pos], section_sems, step, in_section(step)
+        )
+        copy.start()
+        section_copies.append(copy)
+    section_slots[section_pos] = one_square[...]
+
+    row_copies = []
+    for step in range(1, tensors_n):
+        peer = lax.rem(tensor_pos + step, tensors_n)
+        copy = remote(rows_ref.at[peer], row_slots.at[step], row_sems, step, {"tensor": peer})
+        copy.start()
+        row_copies.append(copy)
+
+    for copy in section_copies:
+        copy.wait_recv()
+    total = section_slots[0]
+    for k in range(1, sections_n):
+        total = total + section_slots[k]
+    group_square[...] = total
+    group_copies = []
+    for step in range(1, group_n):
+        copy = remote(
+            group_square, group_slots.at[me], group_sems, step, in_group(step)[1]
+        )
+        copy.start()
+        group_copies.append(copy)
+    group_slots[me] = group_square[...]
+    for copy in group_copies:
+        copy.wait_recv()
+    total = group_slots[0]
+    for k in range(1, group_n):
+        total = total + group_slots[k]
+    clip_tile = jnp.minimum(1.0, lax.rsqrt(total / entry_count + clip_eps))
+    clip = clip_tile[0:1, 0:1]
+
+    def dir_copy(c):
+        columns = pl.ds(pl.multiple_of(c * width, width), width)
+        return remote(
+            dir_own.at[:, columns],
+            dir_landed.at[:, columns],
+            dir_sems,
+            c,
+            {"shard": 1 - shard_pos},
+        )
+
+    @pl.loop(0, chunks)
+    def _(c):
+        columns = pl.ds(pl.multiple_of(c * width, width), width)
+        rows = pl.ds(pl.multiple_of(shard_pos * rank_rows, rank_rows), rank_rows)
+        first_new, second_new, direction = adam_direction(
+            clip * proj_ref[c, rows, :], first_ref[:, columns], second_ref[:, columns]
+        )
+        first_out[:, columns] = first_new
+        second_out[:, columns] = second_new
+        dir_own[:, columns] = direction
+        dir_copy(c).start()
+
+    first_new, second_new, direction = adam_direction(
+        clip * gain_ref[shard_pos], gain_first_ref[...], gain_second_ref[...]
+    )
+    gain_first_out[...] = first_new
+    gain_second_out[...] = second_new
+    gain_step_out[...] = direction
+
+    for copy in row_copies:
+        copy.wait_recv()
+    current = rows_ref[tensor_pos]
+    for step in range(1, tensors_n):
+        current = current + row_slots[step]
+    gram[...] = exact_dims(current, current, ((0,), (0,)))
+    gram_copies = []
+    for step in range(1, group_n):
+        peer, where = in_group(step)
+        copy = remote(
+            gram.at[pl.ds(pl.multiple_of(peer * piece, piece), piece), :],
+            gram_slots.at[step],
+            gram_sems,
+            step,
+            where,
+        )
+        copy.start()
+        gram_copies.append(copy)
+    mine = pl.ds(pl.multiple_of(me * piece, piece), piece)
+    summed = gram[mine, :]
+    for step, copy in enumerate(gram_copies):
+        copy.wait_recv()
+        summed = summed + gram_slots[step + 1]
+    gram_part[...] = summed
+    full_copies = []
+    for step in range(1, group_n):
+        copy = remote(gram_part, gram_full.at[mine, :], full_sems, step, in_group(step)[1])
+        copy.start()
+        full_copies.append(copy)
+    gram_full[mine, :] = summed
+    for copy in full_copies:
+        copy.wait_recv()
+    mixer, scale = ns_mixer(gram_full[...])
+    basis_out[...] = exact_dot(current * scale, mixer)
+
+    @pl.loop(0, chunks)
+    def _(c):
+        dir_copy(c).wait_recv()
+        dir_copy(c).wait_send()
+
+    direction_out[shard_pos] = dir_own[...]
+    direction_out[1 - shard_pos] = dir_landed[...]
+    for copies in (section_copies, row_copies, group_copies, gram_copies, full_copies):
+        for copy in copies:
+            copy.wait_send()
+
+
+def finish(axes, proj, rows, square, gain, first, second, gain_first, gain_second):
+    shards_n, tensors_n, sections_n, _ = axes
+    group_n = shards_n * tensors_n
+    chunks, rank, width = proj.shape
+    rank_rows, cols = first.shape
+    f32 = jnp.float32
+    vmem = pl.BlockSpec(memory_space=pltpu.VMEM)
+    shape = jax.ShapeDtypeStruct
+    tile = (8, 128)
+    dma = pltpu.SemaphoreType.DMA
+    return pl.pallas_call(
+        functools.partial(finish_kernel, axes),
+        out_shape=(
+            shape((rank_rows, cols), f32),
+            shape((rank_rows, cols), f32),
+            shape((shards_n, rank_rows, cols), f32),
+            shape((rank, rank), f32),
+            shape(gain_first.shape, f32),
+            shape(gain_first.shape, f32),
+            shape(gain_first.shape, f32),
+        ),
+        in_specs=[vmem] * 8,
+        out_specs=(vmem,) * 7,
+        scratch_shapes=[
+            pltpu.VMEM(rows.shape, f32),
+            pltpu.VMEM(tile, f32),
+            pltpu.VMEM((sections_n,) + tile, f32),
+            pltpu.VMEM(tile, f32),
+            pltpu.VMEM((group_n,) + tile, f32),
+            pltpu.VMEM((rank_rows, cols), f32),
+            pltpu.VMEM((rank_rows, cols), f32),
+            pltpu.VMEM((rank, rank), f32),
+            pltpu.VMEM((group_n, rank // group_n, rank), f32),
+            pltpu.VMEM((rank // group_n, rank), f32),
+            pltpu.VMEM((rank, rank), f32),
+            dma((2, tensors_n)),
+            dma((2, sections_n)),
+            dma((2, group_n)),
+            dma((2, chunks)),
+            dma((2, group_n)),
+            dma((2, group_n)),
+        ],
+        compiler_params=pltpu.CompilerParams(
+            collective_id=1, has_side_effects=True, vmem_limit_bytes=48 * 2**20
+        ),
+        cost_estimate=pl.CostEstimate(flops=2**32, bytes_accessed=2**24, transcendentals=2**20),
+        name="finish",
+    )(proj, rows, square, gain, first, second, gain_first, gain_second)
+
+
+def paired(
+    activations, out_grad, basis, first_moment, second_moment, gain_partial, gain_first, gain_second
+):
+    shards_n = lax.axis_size("shard")
+    tensors_n = lax.axis_size("tensor")
+    sections_n = lax.axis_size("section")
+    rows_here = basis.shape[1]
+    rank = basis.shape[2]
+    cols = out_grad.shape[2]
+    basis_here = basis[0]
+    gain = gain_partial[0, 0].reshape(shards_n, 8, rows_here // 8)
+    proj, rows, square, gain_total = exchange(activations[0], out_grad[0], basis_here.T, gain)
+    axes = (shards_n, tensors_n, sections_n, float(sections_n * (D * FF + D)))
+    gain_shape = (8, rows_here // 8)
+    first, second, direction, new_basis, gain_step, gain_first_new, gain_second_new = finish(
+        axes,
+        proj,
+        rows.reshape(tensors_n, rows_here // tensors_n, rank),
+        square,
+        gain_total,
+        first_moment[0],
+        second_moment[0],
+        gain_first[0].reshape(gain_shape),
+        gain_second[0].reshape(gain_shape),
+    )
+    update = exact_dot(basis_here, direction.reshape(rank, cols))
+    return (
+        update[None],
+        first[None],
+        second[None],
+        new_basis[None],
+        gain_step.reshape(1, rows_here),
+        gain_first_new.reshape(1, rows_here),
+        gain_second_new.reshape(1, rows_here),
+    )
+
+
 def solution(mesh):
     placed = (
         P("section", "shard", None),
@@ -153,8 +599,10 @@
         P("section", "shard"),
         P("section", "shard"),
     )
+    one_layer = mesh.shape["section"] == LAYERS
+    body = paired if mesh.shape["shard"] == 2 and one_layer else shards
     return jax.shard_map(
-        shards,
+        body,
         mesh=mesh,
         in_specs=placed,
         out_specs=(

time: 505 us -> 351 us (0.70)
  waiting for transfers between devices: 336 us -> 0 us
  Pallas kernels: 0 us -> 313 us
  matrix products: 73.9 us -> 17.1 us
  blocking collectives: 44.4 us -> 0 us
  between operations: 16.7 us -> 0.69 us
  other arithmetic: 12.9 us -> 0 us
    pallas_call x0 -> x2, Pallas kernels: none -> 313 us  [the longest x1 241 us: exchange(): pl.pallas_call(exchange_kernel, out_shape=(jax.ShapeDtypeStruct((chunks,...]
    reduce_scatter x2 -> x0, waiting for transfers between devices: 192 us -> none  [the longest x1 192 us: shards(): lax.psum_scatter(row_term(jnp.int32(0), lax.axis_size('shard') * rows_her...]
    psum x2 -> x0, waiting for transfers between devices: 118 us -> none  [the longest x1 62.9 us: shards(): lax.psum((part_proj, gain_partial[layer_index, 0]), 'shard')]
    dot_general x5 -> x0, matrix products: 64 us -> none  [the longest x1 24.3 us: row_term(): lax.dot_general(tokens_in, grads_out, (((0,), (0,)), ((), ())), preferred...]
    psum x2 -> x0, blocking collectives: 44.4 us -> none  [the longest x1 39.4 us: shards(): total_sq = lax.psum(square_sum, ('shard', 'tensor', 'section'))]
    all_gather x1 -> x0, waiting for transfers between devices: 25.8 us -> none  [shards(): lax.all_gather(direction, 'shard', axis=0, tiled=True)]
    reduce_sum x3 -> x0, other arithmetic: 8.38 us -> none  [the longest x1 6.19 us: shards(): square_sum = jnp.sum(grad_block * grad_block)]
    dot_general x18 -> x1, matrix products: 9.84 us -> 17.1 us  [exact_dot(): return jnp.dot(left, right, precision=exact_mode)]
  transfers between devices with their start and end apart: 5 -> 0, of which waited for: 4 -> 0; matrix products, arithmetic and copies ran while one was open for 9% -> 0% of each run, Pallas kernels for 0% -> 0%
where the time goes in v2:
time: 351 us
  Pallas kernels  313 us (89%)
  local copies, waits for them, and re-layouts  19.9 us (6%)
  matrix products  17.1 us (5%)
    pallas_call x1, Pallas kernels, exchange(): pl.pallas_call(exchange_kernel, out_shape=(jax.ShapeDtypeStruct((chunks,...  241 us
    pallas_call x1, Pallas kernels, finish(): pl.pallas_call(functools.partial(finish_kernel, axes), out_shape=(shape((...  72.3 us
    unnamed x22, local copies, waits for them, and re-layouts  19.9 us
    dot_general x1, matrix products, exact_dot(): return jnp.dot(left, right, precision=exact_mode)  17.1 us

profile of v2, /device:TPU:0, one launch (start us, length us, event | category | flops | bytes accessed | tf_op | source)
XLA Modules:
  0.0 350.5 jit_solution(2365156624396722888)
XLA Ops:
  0.6 2.5 copy.15
  3.2 0.0 copy-start
  3.2 0.0 copy-start.2
  3.2 0.0 copy-start.3
  3.2 240.5 %exchange.1 = (f32[8,256,256]{2,1,0:T(8,128)}, f32[1024,256]{1,0:T(8,128)}, f32[8,256]{1,0:T(8,128)}, f32[2,8,128]{2,1,0:T(8,128)}) custom-call(bf16[2048,2048]{1,0:T(8,128)(2,1)} %bitcast.39, bf16[2048,2048]{1,0:T(8,128)(2,1)} %bitcast.40, f32[256,1024]{1,0:T(8,128)} %bitcast.38, f32[2,8,128]{2,1,0:T(8,128)} %bitcast.41), custom_call_target="tpu_custom_call" | custom-call | flops 30064771072 | bytes 33554432 | tf_op jit(solution)/shard_map/exchange/pallas_call | solution.py:285
  243.7 0.0 copy-done
  243.7 0.0 copy-done.2
  243.7 0.0 copy-done.3
  243.7 0.0 copy-start.1
  243.7 1.2 copy-done.1
  244.9 0.0 copy-start.4
  245.0 1.2 copy-done.4
  246.2 0.0 copy-start.5
  246.2 0.7 copy-done.5
  246.9 0.7 copy-done.6
  247.6 72.3 %finish.1 = (f32[128,2048]{1,0:T(8,128)S(1)}, f32[128,2048]{1,0:T(8,128)S(1)}, f32[2,128,2048]{2,1,0:T(8,128)}, f32[256,256]{1,0:T(8,128)S(1)}, f32[8,128]{1,0:T...) custom-call(f32[8,256,256]{2,1,0:T(8,128)} %get-tuple-element.18.proj_ref, f32[4,256,256]{2,1,0:T(8,128)S(1)} %bitcast.36, ...), custom_call_target="tpu_custom_call" | custom-call | flops 4294967296 | bytes 16777216 | tf_op jit(solution)/shard_map/finish/pallas_call | solution.py:514
  319.8 17.1 %convolution_bitcast_fusion = f32[1,1024,2048]{1,2,0:T(8,128)} fusion(f32[256,2048]{1,0:T(8,128)} %bitcast.37, f32[1,1024,256]{2,1,0:T(8,128)} %param.10), kind=kOutput, calls=%fused_computation | convolution fusion | flops 6442450944 | bytes 11534336 | tf_op jit(solution)/shard_map/dot_general | solution.py:40
  337.0 9.1 %copy.16 = f32[1,1024,2048]{2,1,0:T(8,128)} copy(f32[1,1024,2048]{1,2,0:T(8,128)} %convolution_bitcast_fusion) | data formatting | bytes 16777216
  346.1 1.0 copy.23
  347.1 1.0 copy.24
  348.0 0.7 copy.25
  348.7 0.6 copy.26
  349.3 0.6 copy.27
  349.9 0.6 copy.28
  (1 shorter events, 0.0 us)
Async XLA Ops:
  3.2 240.5 %copy-start = (f32[1,128,2048]{2,1,0:T(8,128)S(1)}, f32[1,128,2048]{2,1,0:T(8,128)}, u32[]{:S(2)}) copy-start(f32[1,128,2048]{2,1,0:T(8,128)} %param.11) | copy-start | bytes 3145732
  3.2 240.5 %copy-start.2 = (f32[1,1024]{1,0:T(1,128)S(1)}, f32[1,1024]{1,0:T(1,128)}, u32[]{:S(2)}) copy-start(f32[1,1024]{1,0:T(1,128)} %param.14) | copy-start | bytes 12292
  3.2 240.5 %copy-start.3 = (f32[1,1024]{1,0:T(1,128)S(1)}, f32[1,1024]{1,0:T(1,128)}, u32[]{:S(2)}) copy-start(f32[1,1024]{1,0:T(1,128)} %param.15) | copy-start | bytes 12292
  243.7 1.2 copy-start.1
  244.9 1.2 copy-start.4
  246.2 0.7 copy-start.5
  246.9 0.7 copy-start.6

commit v3 on v2

--- a/solution.py
+++ b/solution.py
@@ -159,14 +159,16 @@
 
 
 def exchange_kernel(
-    tokens_ref,
-    grads_ref,
+    tokens_hbm,
+    grads_hbm,
     basis_t_ref,
     gain_ref,
     proj_ref,
     rows_ref,
     square_ref,
     gain_out_ref,
+    tokens_ref,
+    grads_ref,
     sent,
     landed,
     own,
@@ -179,10 +181,32 @@
     part_recv,
     gain_send,
     gain_recv,
+    token_sems,
+    column_sems,
 ):
     chunks, rows_here, width = own.shape
     me = lax.axis_index("shard")
     other = 1 - me
+
+    def token_copy(half, k):
+        rows = pl.ds(pl.multiple_of(half * rows_here, rows_here), rows_here)
+        return pltpu.make_async_copy(
+            tokens_hbm.at[:, rows], tokens_ref.at[:, rows], token_sems.at[k]
+        )
+
+    def column_copy(c):
+        columns = pl.ds(pl.multiple_of(c * width, width), width)
+        return pltpu.make_async_copy(
+            grads_hbm.at[:, columns], grads_ref.at[:, columns], column_sems.at[c]
+        )
+
+    token_copy(other, 0).start()
+
+    @pl.loop(0, chunks)
+    def _(c):
+        column_copy(c).start()
+
+    token_copy(me, 1).start()
     barrier = pltpu.get_barrier_semaphore()
     pl.semaphore_signal(barrier, inc=1, device_id={"shard": other}, device_id_type=MESH)
     pl.semaphore_wait(barrier, 1)
@@ -219,10 +243,15 @@
                 preferred_element_type=jnp.float32,
             )
 
+    token_copy(other, 0).wait()
+
     @pl.loop(0, chunks)
     def _(c):
+        column_copy(c).wait()
         multiply(sent, other, c)
         grad_copy(c).start()
+
+    token_copy(me, 1).wait()
 
     @pl.loop(0, chunks)
     def _(c):
@@ -290,9 +319,11 @@
             jax.ShapeDtypeStruct((8, CHUNK), f32),
             jax.ShapeDtypeStruct(gain.shape, f32),
         ),
-        in_specs=[vmem] * 4,
+        in_specs=[pl.BlockSpec(memory_space=pl.ANY)] * 2 + [vmem] * 2,
         out_specs=(vmem,) * 4,
         scratch_shapes=[
+            pltpu.VMEM(tokens_in.shape, tokens_in.dtype),
+            pltpu.VMEM(grads_out.shape, grads_out.dtype),
             pltpu.VMEM((chunks, rows_here, CHUNK), f32),
             pltpu.VMEM((chunks, rows_here, CHUNK), f32),
             pltpu.VMEM((chunks, rows_here, CHUNK), f32),
@@ -305,6 +336,8 @@
             pltpu.SemaphoreType.DMA((chunks,)),
             pltpu.SemaphoreType.DMA,
             pltpu.SemaphoreType.DMA,
+            pltpu.SemaphoreType.DMA((2,)),
+            pltpu.SemaphoreType.DMA((chunks,)),
         ],
         compiler_params=pltpu.CompilerParams(
             collective_id=0, has_side_effects=True, vmem_limit_bytes=60 * 2**20
@@ -320,8 +353,8 @@
     rows_ref,
     square_ref,
     gain_ref,
-    first_ref,
-    second_ref,
+    first_hbm,
+    second_hbm,
     gain_first_ref,
     gain_second_ref,
     first_out,
@@ -348,6 +381,9 @@
     dir_sems,
     gram_sems,
     full_sems,
+    first_ref,
+    second_ref,
+    moment_sems,
 ):
     shards_n, tensors_n, sections_n, entry_count = axes
     group_n = shards_n * tensors_n
@@ -358,6 +394,10 @@
     section_pos = lax.axis_index("section")
     me = shard_pos * tensors_n + tensor_pos
     piece = rank // group_n
+    first_copy = pltpu.make_async_copy(first_hbm, first_ref, moment_sems.at[0])
+    second_copy = pltpu.make_async_copy(second_hbm, second_ref, moment_sems.at[1])
+    first_copy.start()
+    second_copy.start()
 
     def in_group(step):
         peer = lax.rem(me + step, group_n)
@@ -424,6 +464,9 @@
         total = total + group_slots[k]
     clip_tile = jnp.minimum(1.0, lax.rsqrt(total / entry_count + clip_eps))
     clip = clip_tile[0:1, 0:1]
+
+    first_copy.wait()
+    second_copy.wait()
 
     def dir_copy(c):
         columns = pl.ds(pl.multiple_of(c * width, width), width)
@@ -522,7 +565,7 @@
             shape(gain_first.shape, f32),
             shape(gain_first.shape, f32),
         ),
-        in_specs=[vmem] * 8,
+        in_specs=[vmem] * 4 + [pl.BlockSpec(memory_space=pl.ANY)] * 2 + [vmem] * 2,
         out_specs=(vmem,) * 7,
         scratch_shapes=[
             pltpu.VMEM(rows.shape, f32),
@@ -542,6 +585,9 @@
             dma((2, chunks)),
             dma((2, group_n)),
             dma((2, group_n)),
+            pltpu.VMEM(first.shape, f32),
+            pltpu.VMEM(second.shape, f32),
+            dma((2,)),
         ],
         compiler_params=pltpu.CompilerParams(
             collective_id=1, has_side_effects=True, vmem_limit_bytes=48 * 2**20
@@ -549,6 +595,51 @@
         cost_estimate=pl.CostEstimate(flops=2**32, bytes_accessed=2**24, transcendentals=2**20),
         name="finish",
     )(proj, rows, square, gain, first, second, gain_first, gain_second)
+
+
+def split(value):
+    high = value.astype(jnp.bfloat16)
+    return high, (value - high.astype(jnp.float32)).astype(jnp.bfloat16)
+
+
+def apply_kernel(basis_ref, direction_ref, *refs):
+    count = len(refs) // 2
+    left_high, left_low = split(basis_ref[...])
+    right_high, right_low = split(direction_ref[...])
+
+    def term(left, right):
+        return jnp.dot(left, right, preferred_element_type=jnp.float32)
+
+    refs[count][...] = (
+        term(left_low, right_high) + term(left_high, right_low) + term(left_high, right_high)
+    )
+    for source, target in zip(refs[:count], refs[count + 1 :]):
+        target[...] = source[...]
+
+
+def apply_direction(basis_here, direction, moments, rest):
+    rows_here, rank = basis_here.shape
+    cols = direction.shape[1]
+    f32 = jnp.float32
+
+    def by_column(shape):
+        return pl.BlockSpec((shape[0], CHUNK), lambda c: (0, c))
+
+    def whole(shape):
+        return pl.BlockSpec(shape, lambda c: (0, 0))
+
+    passed = [by_column(a.shape) for a in moments] + [whole(a.shape) for a in rest]
+    arrays = list(moments) + list(rest)
+    shape = jax.ShapeDtypeStruct
+    return pl.pallas_call(
+        apply_kernel,
+        grid=(cols // CHUNK,),
+        out_shape=[shape((rows_here, cols), f32)] + [shape(a.shape, f32) for a in arrays],
+        in_specs=[whole(basis_here.shape), by_column(direction.shape)] + passed,
+        out_specs=[by_column((rows_here, cols))] + passed,
+        compiler_params=pltpu.CompilerParams(vmem_limit_bytes=32 * 2**20),
+        name="apply_direction",
+    )(basis_here, direction, *arrays)
 
 
 def paired(
@@ -576,7 +667,12 @@
         gain_first[0].reshape(gain_shape),
         gain_second[0].reshape(gain_shape),
     )
-    update = exact_dot(basis_here, direction.reshape(rank, cols))
+    update, first, second, new_basis, gain_step, gain_first_new, gain_second_new = apply_direction(
+        basis_here,
+        direction.reshape(rank, cols),
+        (first, second),
+        (new_basis, gain_step, gain_first_new, gain_second_new),
+    )
     return (
         update[None],
         first[None],

time: 351 us -> 326 us (0.929)
  matrix products: 17.1 us -> 0 us
  local copies, waits for them, and re-layouts: 19.9 us -> 6.83 us
  Pallas kernels: 313 us -> 318 us
    dot_general x1 -> x0, matrix products: 17.1 us -> none  [exact_dot(): return jnp.dot(left, right, precision=exact_mode)]
    unnamed x22 -> x18, local copies, waits for them, and re-layouts: 19.9 us -> 4.3 us
    pallas_call x0 -> x1, Pallas kernels: none -> 7.32 us  [apply_direction(): pl.pallas_call(apply_kernel, grid=(cols // CHUNK,), out_shape=[shape((row...]
where the time goes in v3:
time: 326 us; the launch traced here: 325 us
  Pallas kernels  318 us (98%)
  local copies, waits for them, and re-layouts  6.83 us (2%)
    pallas_call x1, Pallas kernels, exchange(): pl.pallas_call(exchange_kernel, out_shape=(jax.ShapeDtypeStruct((chunks,...  239 us
    pallas_call x1, Pallas kernels, finish(): pl.pallas_call(functools.partial(finish_kernel, axes), out_shape=(shape((...  71.9 us
    pallas_call x1, Pallas kernels, apply_direction(): pl.pallas_call(apply_kernel, grid=(cols // CHUNK,), out_shape=[shape((row...  7.32 us

profile of v3, /device:TPU:0, one launch (start us, length us, event | category | flops | bytes accessed | tf_op | source)
XLA Modules:
  0.0 325.5 jit_solution(9263043979629489704)
XLA Ops:
  0.6 2.5 copy.15.basis_t_ref
  3.2 0.0 copy-start.2
  3.2 0.0 copy-start.3
  3.2 0.0 copy-start.4
  3.2 0.0 copy-start.5
  3.2 238.7 %exchange.1 = (f32[8,256,256]{2,1,0:T(8,128)}, f32[1024,256]{1,0:T(8,128)}, f32[8,256]{1,0:T(8,128)}, f32[2,8,128]{2,1,0:T(8,128)}) custom-call(bf16[2048,2048]{1,0:T(8,128)(2,1)} %bitcast.27, bf16[2048,2048]{1,0:T(8,128)(2,1)} %bitcast.28, f32[256,1024]{1,0:T(8,128)} %copy.15.basis_t_ref, f32[2,8,128]{2,1,0:T(8,128)} %bitcast.33), custom_call_target="tpu_custom_call" | custom-call | flops 30064771072 | bytes 33554432 | tf_op jit(solution)/shard_map/exchange/pallas_call | solution.py:314
  241.9 0.0 copy-start
  241.9 0.0 copy-done.2
  241.9 0.0 copy-done.3
  242.0 0.0 copy-done.4
  242.0 0.0 copy-done.5
  242.0 0.0 copy-start.6
  242.0 1.3 copy-done.6
  243.3 0.0 copy-start.7
  243.3 0.7 copy-done.7
  244.0 0.0 copy-start.8
  244.0 0.7 copy-done.8
  244.7 71.9 %finish.1 = (f32[128,2048]{1,0:T(8,128)S(1)}, f32[128,2048]{1,0:T(8,128)S(1)}, f32[2,128,2048]{2,1,0:T(8,128)}, f32[256,256]{1,0:T(8,128)S(1)}, f32[8,128]{1,0:T...) custom-call(f32[8,256,256]{2,1,0:T(8,128)} %get-tuple-element.25.proj_ref, f32[4,256,256]{2,1,0:T(8,128)S(1)} %bitcast.26, ...), custom_call_target="tpu_custom_call" | custom-call | flops 4294967296 | bytes 16777216 | tf_op jit(solution)/shard_map/finish/pallas_call | solution.py:557
  316.6 0.0 copy-done
  316.6 0.0 copy-start.1
  316.6 1.6 copy-done.1
  318.2 7.3 %apply_direction.1 = (f32[1024,2048]{1,0:T(8,128)}, f32[128,2048]{1,0:T(8,128)}, f32[128,2048]{1,0:T(8,128)}, f32[256,256]{1,0:T(8,128)}, f32[8,128]{1,0:T(8,128)}, /*index=5*/f32[8,128]{1,0:T(8,128)}, f32[8,128]{1,0:T(8,128)}) custom-call(f32[1024,256]{1,0:T(8,128)S(1)} %bitcast.20, f32[256,2048]{1,0:T(8,128)S(1)} %bitcast.21, ...), custom_call_target="tpu_custom_call" | custom-call | tf_op jit(solution)/shard_map/apply_direction/pallas_call | solution.py:634
Async XLA Ops:
  3.2 238.8 %copy-start.2 = (f32[1,128,2048]{2,1,0:T(8,128)S(1)}, f32[1,128,2048]{2,1,0:T(8,128)}, u32[]{:S(2)}) copy-start(f32[1,128,2048]{2,1,0:T(8,128)} %param.11) | copy-start | bytes 3145732
  3.2 238.8 %copy-start.3 = (f32[1,128,2048]{2,1,0:T(8,128)S(1)}, f32[1,128,2048]{2,1,0:T(8,128)}, u32[]{:S(2)}) copy-start(f32[1,128,2048]{2,1,0:T(8,128)} %param.12) | copy-start | bytes 3145732
  3.2 238.8 %copy-start.4 = (f32[1,1024]{1,0:T(1,128)S(1)}, f32[1,1024]{1,0:T(1,128)}, u32[]{:S(2)}) copy-start(f32[1,1024]{1,0:T(1,128)} %param.14) | copy-start | bytes 12292
  3.2 238.8 %copy-start.5 = (f32[1,1024]{1,0:T(1,128)S(1)}, f32[1,1024]{1,0:T(1,128)}, u32[]{:S(2)}) copy-start(f32[1,1024]{1,0:T(1,128)} %param.15) | copy-start | bytes 12292
  241.9 74.6 %copy-start = (f32[1,1024,256]{2,1,0:T(8,128)S(1)}, f32[1,1024,256]{2,1,0:T(8,128)}, u32[]{:S(2)}) copy-start(f32[1,1024,256]{2,1,0:T(8,128)} %param.10) | copy-start | bytes 3145732
  242.0 1.3 copy-start.6
  243.3 0.7 copy-start.7
  244.0 0.7 copy-start.8
  316.6 1.6 copy-start.1
